TPU v7x, 256 devices: a whole 4x4x8 slice. The times are simulated.
256 devices in a mesh: dp: 32 (over z, y), mp: 8 (over x, core).
Axes of the slice: x: 4, y: 4, z: 8, core: 2. Of those that a mesh axis runs over, the one named last changes fastest.
Arguments:
- queries_vec: bfloat16 [128, 64, 2048], P('dp', None, 'mp')
- retr_query: bfloat16 [128, 4096], P('dp', 'mp'), may hold values from -6 to 6
- passages: bfloat16 [256, 64, 4096], P('dp', None, 'mp'), may hold values from -6 to 6
- kv_weight: bfloat16 [4096, 2, 2048], P(None, None, 'mp'), may hold values from -0.09375 to 0.09375
- retrieval: int32 [128, 8], replicated, may hold values from 0 to 255, as said below
- lengths: int32 [256], replicated, may hold values from 8 to 64, as said below
- ctx_cot: bfloat16 [128, 64, 2048], P('dp', None, 'mp'), may hold values from -6 to 6
Outputs:
- context: bfloat16 [128, 64, 2048], P('dp', None, 'mp')
- divergence: float32 [128], P('dp')
- grad_passages: bfloat16 [256, 64, 4096], P('dp', None, 'mp')
Inputs may be any that keep to these rules, and one draw needn't show every extreme that they name: `retrieval`: each query's 8 ids differ; within the 4 queries of one index of dp (aligned blocks of 4 rows) no id repeats, and at most 2 of their ids share an owner (id // 8), exactly 2 for some owner in every block. `lengths`: multiples of 8.
All inputs are finite; a program needn't handle non-finite values.
Results may differ from a plain program's by a relative error of at most 0.015.
Values may be sent and summed in bfloat16 or wider, within the bound.
No kernel may reach another device: no remote copies, remote signals or barrier semaphores. Data moves between devices by JAX's collectives and lax.ppermute only.
A program may use at most 64 MiB of HBM per device.

v0:
```python
import jax
import jax.numpy as jnp
from jax import lax
from jax.sharding import PartitionSpec as P

HEADS = 32
HD = 64


INV_TEMP = 8.0
DISTILL = 128.0


def per_device(queries_vec, retr_query, passages, kv_weight, retrieval, lengths, ctx_cot):
    groups = lax.axis_size("dp")
    my_group = lax.axis_index("dp")
    own_count = passages.shape[0]
    token_count = passages.shape[1]
    local_width = passages.shape[2]
    full_width = kv_weight.shape[0]
    head_cols = kv_weight.shape[2]
    local_heads = head_cols // HD
    query_count = queries_vec.shape[0]
    query_tokens = queries_vec.shape[1]
    picks = retrieval.shape[1]
    group_rows = query_count * picks
    capacity = max(2, (group_rows + groups - 1) // groups)
    score_scale = HD ** (-0.5)
    width_scale = INV_TEMP * full_width ** (-0.5)
    owner_ids = (retrieval // own_count).reshape(groups, group_rows)
    local_ids = (retrieval % own_count).reshape(groups, group_rows)
    row_index = jnp.arange(group_rows, dtype=jnp.int32)
    earlier = row_index[:, None] > row_index[None, :]
    same_owner = owner_ids[:, :, None] == owner_ids[:, None, :]
    ranks = jnp.sum(same_owner & earlier[None], axis=2)
    slot_range = jnp.arange(capacity, dtype=jnp.int32)
    selected = (owner_ids[:, None, :] == my_group) & (
        ranks[:, None, :] == slot_range[None, :, None]
    )
    send_local = jnp.sum(jnp.where(selected, local_ids[:, None, :], 0), axis=2)
    send_valid = jnp.any(selected, axis=2)
    own_lengths = lax.dynamic_slice_in_dim(lengths, my_group * own_count, own_count)
    positions = jnp.arange(token_count, dtype=jnp.int32)
    own_valid = positions[None, :] < own_lengths[:, None]
    own_len_f = own_lengths.astype(jnp.float32)
    pooled = jnp.einsum(
        "pt,ptd->pd", own_valid.astype(jnp.bfloat16), passages, preferred_element_type=jnp.float32
    )
    pooled = (pooled / own_len_f[:, None]).astype(jnp.bfloat16)
    projected = jnp.einsum(
        "ptd,dkc->ptkc",
        lax.all_gather(passages, "mp", axis=2, tiled=True),
        kv_weight,
        preferred_element_type=jnp.float32,
    ).astype(jnp.bfloat16)
    keep = send_valid.astype(jnp.bfloat16)
    send_rows = projected[send_local] * keep[:, :, None, None, None]
    send_pool = pooled[send_local] * keep[:, :, None]
    recv_rows, recv_pool = (
        lax.all_to_all(send_rows, "dp", split_axis=0, concat_axis=0, tiled=True),
        lax.all_to_all(send_pool, "dp", split_axis=0, concat_axis=0, tiled=True),
    )
    my_owners = lax.dynamic_index_in_dim(owner_ids, my_group, 0, keepdims=False)
    my_ranks = lax.dynamic_index_in_dim(ranks, my_group, 0, keepdims=False)
    my_slots = my_owners * capacity + my_ranks
    my_picks = lax.dynamic_slice_in_dim(retrieval, my_group * query_count, query_count)
    rows_in = recv_rows.reshape(groups * capacity, token_count, 2, head_cols)[my_slots]
    pool_in = recv_pool.reshape(groups * capacity, local_width)[my_slots].reshape(
        query_count, picks, local_width
    )
    score_part = jnp.einsum("qkd,qd->qk", pool_in, retr_query, preferred_element_type=jnp.float32)
    score_sum = lax.psum(score_part, "mp")
    key_span = picks * token_count
    pick_lengths = lengths[my_picks]
    key_mask = (
        (positions[None, None, :] < pick_lengths[:, :, None])
        .astype(jnp.float32)
        .reshape(query_count, key_span)
    )
    rows_in = rows_in.reshape(query_count, key_span, 2, local_heads, HD)
    key_heads = rows_in[:, :, 0]
    value_heads = rows_in[:, :, 1]
    query_heads = queries_vec.reshape(query_count, query_tokens, local_heads, HD)
    scores = (
        jnp.einsum("qihd,qjhd->qhij", query_heads, key_heads, preferred_element_type=jnp.float32)
        * score_scale
    )
    expd = jnp.exp(scores) * key_mask[:, None, None, :]
    prob = expd / jnp.sum(expd, axis=3, keepdims=True)
    prob_b = prob.astype(jnp.bfloat16)
    context = jnp.einsum("qhij,qjhd->qihd", prob_b, value_heads, preferred_element_type=jnp.float32)
    context = context.astype(jnp.bfloat16).reshape(query_count, query_tokens, head_cols)
    mass_part = jnp.sum(
        prob.reshape(query_count, local_heads, query_tokens, picks, token_count), axis=(1, 2, 4)
    )
    mass_sum = lax.psum(mass_part, "mp")
    mass = mass_sum / (HEADS * query_tokens)
    retr_score = score_sum * width_scale
    log_prob = retr_score - jnp.log(jnp.sum(jnp.exp(retr_score), axis=1, keepdims=True))
    divergence = jnp.sum(mass * (jnp.log(mass) - log_prob), axis=1)
    d_score = DISTILL * (jnp.exp(log_prob) - mass)
    pool_grad = (
        (d_score * width_scale)[:, :, None] * retr_query.astype(jnp.float32)[:, None, :]
    ).astype(jnp.bfloat16)
    cot_heads = ctx_cot.reshape(query_count, query_tokens, local_heads, HD)
    d_prob = jnp.einsum(
        "qihd,qjhd->qhij", cot_heads, value_heads, preferred_element_type=jnp.float32
    )
    d_scores = prob * (d_prob - jnp.sum(prob * d_prob, axis=3, keepdims=True)) * score_scale
    d_scores = d_scores.astype(jnp.bfloat16)
    key_grad = jnp.einsum(
        "qhij,qihd->qjhd", d_scores, query_heads, preferred_element_type=jnp.float32
    )
    value_grad = jnp.einsum(
        "qhij,qihd->qjhd", prob_b, cot_heads, preferred_element_type=jnp.float32
    )
    row_grad = jnp.stack(
        [
            key_grad.reshape(group_rows, token_count, head_cols),
            value_grad.reshape(group_rows, token_count, head_cols),
        ],
        axis=2,
    ).astype(jnp.bfloat16)
    back_rows = (
        jnp.zeros((groups * capacity, token_count, 2, head_cols), jnp.bfloat16)
        .at[my_slots]
        .set(row_grad)
    )
    back_rows = back_rows.reshape(groups, capacity, token_count, 2, head_cols)
    back_pool = (
        jnp.zeros((groups * capacity, local_width), jnp.bfloat16)
        .at[my_slots]
        .set(pool_grad.reshape(group_rows, local_width))
        .reshape(groups, capacity, local_width)
    )
    ret_rows, ret_pool = (
        lax.all_to_all(back_rows, "dp", split_axis=0, concat_axis=0, tiled=True),
        lax.all_to_all(back_pool, "dp", split_axis=0, concat_axis=0, tiled=True),
    )
    owner_hot = (
        send_local[:, :, None] == jnp.arange(own_count, dtype=jnp.int32)[None, None, :]
    ) & send_valid[:, :, None]
    owner_hot = owner_hot.astype(jnp.bfloat16).reshape(groups * capacity, own_count)
    grad_rows = jnp.einsum(
        "sp,stkc->ptkc",
        owner_hot,
        ret_rows.reshape(groups * capacity, token_count, 2, head_cols),
        preferred_element_type=jnp.float32,
    ).astype(jnp.bfloat16)
    grad_pool = jnp.einsum(
        "sp,sd->pd",
        owner_hot,
        ret_pool.reshape(groups * capacity, local_width),
        preferred_element_type=jnp.float32,
    )
    partial_grad = jnp.einsum(
        "ptkc,dkc->ptd", grad_rows, kv_weight, preferred_element_type=jnp.float32
    )
    reader_grad = lax.psum_scatter(partial_grad, "mp", scatter_dimension=2, tiled=True)
    retr_grad = (
        own_valid.astype(jnp.float32)[:, :, None] / own_len_f[:, None, None] * grad_pool[:, None, :]
    )
    grad_passages = (reader_grad + retr_grad).astype(jnp.bfloat16)
    return (context, divergence, grad_passages)


def solution(mesh):
    in_specs = (
        P("dp", None, "mp"),
        P("dp", "mp"),
        P("dp", None, "mp"),
        P(None, None, "mp"),
        P(),
        P(),
        P("dp", None, "mp"),
    )
    out_specs = (P("dp", None, "mp"), P("dp"), P("dp", None, "mp"))
    return jax.shard_map(
        per_device, mesh=mesh, in_specs=in_specs, out_specs=out_specs, check_vma=False
    )
```

profile of v0, /device:TPU:1, one launch (start us, length us, event | category | flops | bytes accessed | tf_op | source)
XLA Modules:
  0.0 400.6 jit_solution(1147062476246846815)
XLA Ops:
  10.4 38.4 %all-gather.2.cloned.1.call-done = bf16[8,64,4096]{2,1,0:T(8,128)(2,1)} async-done(((bf16[8,64,512]{2,1,0:T(8,128)(2,1)}), bf16[8,64,4096]{2,1,0:T(8,128)(2,1)}) %all-gather.2.cloned.1.call-update) | async-done | bytes 4194320 | tf_op jit(solution)/shard_map/all_gather | solution.py:52
  48.7 5.8 %fusion.19 = bf16[8,64,2,256]{3,1,2,0:T(8,128)(2,1)S(1)} fusion(bf16[4096,2,256]{2,1,0:T(2,128)(2,1)} %param.10, bf16[8,64,4096]{2,1,0:T(8,128)(2,1)} %all-gather.2.cloned.1.call-done), kind=kOutput, calls=%fused_computation.33 | convolution fusion | flops 2147745792 | bytes 8912896 | tf_op jit(solution)/shard_map/ptd,dkc->ptkc/dot_general | solution.py:50
  54.5 2.8 gather_fusion
  57.3 4.5 %broadcast_multiply_fusion = bf16[32,2,64,2,256]{4,2,3,1,0:T(8,128)(2,1)} fusion(bf16[32,2,64,2,256]{4,2,3,1,0:T(8,128)(2,1)} %bitcast.131, bf16[32,2]{1,0:T(8,128)(2,1)S(1)} %copy.110), kind=kLoop, calls=%fused_computation.26 | loop fusion | flops 2097152 | bytes 8388736 | tf_op jit(solution)/shard_map/mul | solution.py:57
  61.8 9.8 %all-to-all-start = ((bf16[32,2,64,2,256]{4,2,3,1,0:T(8,128)(2,1)}), bf16[32,2,64,2,256]{4,2,3,1,0:T(8,128)(2,1)}, u32[]{:S(2)}, u32[]{:S(2)}) async-start(bf16[32,2,64,2,256]{4,2,3,1,0:T(8,128)(2,1)} %broadcast_multiply_fusion), calls=%async_computation | async-start | bytes 8388608 | tf_op jit(solution)/shard_map/all_to_all | solution.py:60
  73.4 91.7 %all-to-all-done = bf16[32,2,64,2,256]{4,2,3,1,0:T(8,128)(2,1)} async-done(((bf16[32,2,64,2,256]{4,2,3,1,0:T(8,128)(2,1)}), bf16[32,2,64,2,256]{4,2,3,1,0:T(8,128)(2,1)}, u32[]{:S(2)}, u32[]{:S(2)}) %all-to-all-start) | async-done | bytes 4194336 | tf_op jit(solution)/shard_map/all_to_all | solution.py:60
  165.1 2.9 gather_fusion.1
  168.0 6.8 %copy.111 = bf16[32,64,2,256]{1,0,3,2:T(8,128)(2,1)} copy(bf16[32,64,2,256]{3,1,2,0:T(8,128)(2,1)S(1)} %gather_fusion.1) | data formatting | bytes 4194304 | tf_op jit(solution)/shard_map/gather | solution.py:67
  174.8 5.8 %reshape.186 = bf16[4,512,2,4,64]{1,0,4,3,2:T(4,128)(2,1)S(1)} reshape(bf16[32,64,2,256]{1,0,3,2:T(8,128)(2,1)} %copy.111) | data formatting | bytes 4194304 | tf_op jit(solution)/shard_map/reshape | solution.py:80
  181.4 1.9 fusion.29
  183.3 0.8 bitcast_reduce_fusion
  184.1 1.7 fusion.14
  185.8 9.0 %fusion.15 = bf16[4,512,4,64]{1,3,2,0:T(8,128)(2,1)} fusion(bf16[4,64,4,64]{1,3,2,0:T(8,128)(2,1)S(1)} %bitcast.133, f32[4,4,512,64]{2,3,1,0:T(8,128)} %fusion.29, f32[4,4,512,64]{2,3,1,0:T(8,128)S(1)} %get-tuple-element.32, f32[4,4,64]{2,1,0:T(4,128)S(1)} %get-tuple-element.31, f32[4,512]{1,0:T(4,128)S(1)} %compare_convert_fusion), kind=kOutput, calls=%fused_computation.31 | convolution fusion | flops 73401856 | bytes 5386240 | tf_op jit(solution)/shard_map/qhij,qihd->qjhd/dot_general | solution.py:111
  194.8 2.1 copy.121
  196.9 1.8 copy.119
  198.7 3.0 stack_reshape.8
  201.7 2.0 stack_reshape.9
  203.8 4.5 %pad_maximum_fusion = bf16[32,64,2,256]{1,0,3,2:T(8,128)(2,1)} fusion(bf16[32,64,1,256]{1,0,3,2:T(8,128)(2,1)} %stack_reshape.9, bf16[32,64,1,256]{1,0,3,2:T(8,128)(2,1)S(1)} %stack_reshape.8), kind=kLoop, calls=%fused_computation.9 | loop fusion | flops 1048576 | bytes 4194304 | tf_op jit(solution)/shard_map/stack | solution.py:117
  208.3 4.5 %copy.122 = bf16[32,64,2,256]{3,1,2,0:T(8,128)(2,1)S(1)} copy(bf16[32,64,2,256]{1,0,3,2:T(8,128)(2,1)} %pad_maximum_fusion) | data formatting | bytes 4194304 | tf_op jit(solution)/shard_map/stack | solution.py:117
  212.7 2.5 broadcast_in_dim.24
  215.2 5.4 %scatter_fusion = bf16[64,64,2,256]{3,1,2,0:T(8,128)(2,1)} fusion(bf16[64,64,2,256]{3,1,2,0:T(8,128)(2,1)} %broadcast_in_dim.24, s32[32]{0:T(128)S(1)} %fusion.62, bf16[32,64,2,256]{3,1,2,0:T(8,128)(2,1)S(1)} %copy.122), kind=kCustom, calls=%fused_computation.5 | custom fusion | bytes 6291584 | tf_op jit(solution)/shard_map/scatter | solution.py:127
  220.6 8.5 %copy.123 = bf16[32,2,64,2,256]{4,1,3,2,0:T(2,128)(2,1)} copy(bf16[32,2,64,2,256]{4,2,3,1,0:T(8,128)(2,1)} %bitcast.130) | data formatting | bytes 8388608 | tf_op jit(solution)/shard_map/reshape | solution.py:129
  229.1 101.8 %all_to_all.20 = bf16[32,2,64,2,256]{4,1,3,2,0:T(2,128)(2,1)S(1)} all-to-all(bf16[32,2,64,2,256]{4,1,3,2,0:T(2,128)(2,1)} %copy.123), channel_id=1, replica_groups=mesh['dp'=32,'mp'=8] {'dp'}, dimensions={0} | all-to-all | bytes 8388608 | tf_op jit(solution)/shard_map/all_to_all | solution.py:137
  331.0 2.3 fusion.24
  333.3 5.6 %convolution_bitcast_fusion = f32[8,64,4096]{2,1,0:T(8,128)} fusion(bf16[4096,2,256]{2,1,0:T(2,128)(2,1)S(1)} %copy-done.11, bf16[8,64,2,256]{3,0,2,1:T(8,128)(2,1)S(1)} %fusion.24), kind=kOutput, calls=%fused_computation.8 | convolution fusion | flops 2147483648 | bytes 13107200 | tf_op jit(solution)/shard_map/ptkc,dkc->ptd/dot_general | solution.py:156
  341.7 6.7 %all-to-all-start.1 = ((bf16[32,2,512]{2,1,0:T(2,128)(2,1)}), bf16[32,2,512]{2,1,0:T(2,128)(2,1)S(1)}, u32[]{:S(2)}, u32[]{:S(2)}) async-start(bf16[32,2,512]{2,1,0:T(2,128)(2,1)} %broadcast_multiply_fusion.1), calls=%async_computation.1 | async-start | bytes 131072 | tf_op jit(solution)/shard_map/all_to_all | solution.py:61
  348.6 8.8 %all-to-all-done.1 = bf16[32,2,512]{2,1,0:T(2,128)(2,1)S(1)} async-done(((bf16[32,2,512]{2,1,0:T(2,128)(2,1)}), bf16[32,2,512]{2,1,0:T(2,128)(2,1)S(1)}, u32[]{:S(2)}, u32[]{:S(2)}) %all-to-all-start.1) | async-done | bytes 65568 | tf_op jit(solution)/shard_map/all_to_all | solution.py:61
  358.8 14.9 %all-reduce = (f32[4,8]{1,0:T(4,128)S(1)}, f32[4,8]{1,0:T(4,128)S(1)}) all-reduce(f32[4,8]{1,0:T(4,128)S(1)} %reduce_sum.78, f32[4,8]{1,0:T(4,128)S(1)} %bitcast.138), channel_id=1, replica_groups=mesh['dp'=32,'mp'=8] {'mp'}, use_global_device_ids=true, to_apply=%region_6.7 | all-reduce | flops 64 | bytes 512 | tf_op jit(solution)/shard_map/psum | solution.py:96
  376.1 3.9 all-to-all-start.3
  381.6 7.3 %all-to-all-done.3 = bf16[32,2,512]{2,1,0:T(2,128)(2,1)S(1)} async-done(((bf16[32,2,512]{2,1,0:T(2,128)(2,1)}), bf16[32,2,512]{2,1,0:T(2,128)(2,1)S(1)}, u32[]{:S(2)}, u32[]{:S(2)}) %all-to-all-start.3) | async-done | bytes 65568 | tf_op jit(solution)/shard_map/all_to_all | solution.py:138
  389.1 2.5 reduce-scatter.2.cloned.1.call-done
  391.6 2.2 add_convert_fusion
  (84 shorter events, 14.1 us)
Async XLA Ops:
  7.2 41.6 %all-gather.2.cloned.1.call-start = ((), (), s32[]{:S(2)}) async-start(), calls=%async_computation.5 | async-start | bytes 4718592 | tf_op jit(solution)/shard_map/all_gather | solution.py:52
  61.8 9.9 %copy-start.9 = (s32[128,8]{0,1:T(8,128)S(1)}, s32[128,8]{0,1:T(8,128)}, u32[]{:S(2)}) copy-start(s32[128,8]{0,1:T(8,128)} %param.11) | copy-start | bytes 12292
  61.8 10.2 %copy-start = (s32[256]{0:T(256)S(1)}, s32[256]{0:T(256)}, u32[]{:S(2)}) copy-start(s32[256]{0:T(256)} %param.12) | copy-start | bytes 3076
  61.8 103.4 %all-to-all-start = ((bf16[32,2,64,2,256]{4,2,3,1,0:T(8,128)(2,1)}), bf16[32,2,64,2,256]{4,2,3,1,0:T(8,128)(2,1)}, u32[]{:S(2)}, u32[]{:S(2)}) async-start(bf16[32,2,64,2,256]{4,2,3,1,0:T(8,128)(2,1)} %broadcast_multiply_fusion), calls=%async_computation | async-start | bytes 8388608 | tf_op jit(solution)/shard_map/all_to_all | solution.py:60
  71.6 1.4 copy-start.7
  71.6 1.6 copy-start.8
  71.6 319.9 %reduce-scatter.2.cloned.1.call-start = ((), (), s32[]{:S(2)}) async-start(), calls=%async_computation.6 | async-start | bytes 9437184 | tf_op jit(solution)/shard_map/reduce_scatter | solution.py:159
  181.4 2.7 copy-start.3
  184.1 1.7 copy-start.1
  194.8 2.1 copy-start.6
  331.0 2.3 copy-start.11
  338.9 1.0 copy-start.5
  338.9 9.5 %copy-start.10 = (bf16[4,512]{1,0:T(4,128)(2,1)S(1)}, bf16[4,512]{1,0:T(4,128)(2,1)}, u32[]{:S(2)}) copy-start(bf16[4,512]{1,0:T(4,128)(2,1)} %param.8) | copy-start | bytes 12292
  338.9 19.2 %copy-start.2 = (f32[4,4,512,64]{2,3,1,0:T(8,128)S(1)}, f32[4,4,512,64]{2,3,1,0:T(8,128)}, u32[]{:S(2)}) copy-start(f32[4,4,512,64]{2,3,1,0:T(8,128)} %copy-done.1) | copy-start | bytes 6291460
  340.1 39.9 %copy-start.4 = (bf16[4,512,1,4,64]{1,0,4,3,2:T(4,128)(2,1)S(1)}, bf16[4,512,1,4,64]{1,0,4,3,2:T(4,128)(2,1)}, u32[]{:S(2)}) copy-start(bf16[4,512,1,4,64]{1,0,4,3,2:T(4,128)(2,1)} %copy-done.3) | copy-start | bytes 3145732
  341.7 15.7 %all-to-all-start.1 = ((bf16[32,2,512]{2,1,0:T(2,128)(2,1)}), bf16[32,2,512]{2,1,0:T(2,128)(2,1)S(1)}, u32[]{:S(2)}, u32[]{:S(2)}) async-start(bf16[32,2,512]{2,1,0:T(2,128)(2,1)} %broadcast_multiply_fusion.1), calls=%async_computation.1 | async-start | bytes 131072 | tf_op jit(solution)/shard_map/all_to_all | solution.py:61
  376.1 12.7 %all-to-all-start.3 = ((bf16[32,2,512]{2,1,0:T(2,128)(2,1)}), bf16[32,2,512]{2,1,0:T(2,128)(2,1)S(1)}, u32[]{:S(2)}, u32[]{:S(2)}) async-start(bf16[32,2,512]{2,1,0:T(2,128)(2,1)} %reshape.193), calls=%async_computation.4 | async-start | bytes 131072 | tf_op jit(solution)/shard_map/all_to_all | solution.py:138
Sparse Core Ops, SparseCore 0:
  9.8 38.8 all-gather.1
  339.1 52.4 reduce-scatter.1
where the time goes:
time: 402 us; the launch traced here: 401 us
  waiting for transfers between devices  149 us (37%)
  blocking collectives  117 us (29%)
  local copies, waits for them, and re-layouts  55 us (14%)
  matrix products  28.4 us (7%)
  starting transfers between devices  20.5 us (5%)
  other arithmetic  16.3 us (4%)
  between operations  14.3 us (4%)
    all_to_all x1, blocking collectives, per_device(): lax.all_to_all(back_rows, 'dp', split_axis=0, concat_axis=0, tiled=True)  102 us
    all_to_all x1, waiting for transfers between devices, per_device(): lax.all_to_all(send_rows, 'dp', split_axis=0, concat_axis=0, tiled=True)  91.7 us
    all_gather x1, waiting for transfers between devices, per_device(): lax.all_gather(passages, 'mp', axis=2, tiled=True)  38.4 us
    psum x1, blocking collectives, per_device(): mass_sum = lax.psum(mass_part, 'mp')  14.9 us
    all_to_all x1, starting transfers between devices, per_device(): lax.all_to_all(send_rows, 'dp', split_axis=0, concat_axis=0, tiled=True)  9.83 us
    gather x2, local copies, waits for them, and re-layouts, per_device(): recv_rows.reshape(groups * capacity, token_count, 2, head_cols)[my_slots]  9.69 us
    another operation x3, local copies, waits for them, and re-layouts, per_device(): jnp.stack([key_grad.reshape(group_rows, token_count, head_cols), value_gr...  9.48 us
    dot_general x1, matrix products, per_device(): jnp.einsum('qhij,qihd->qjhd', d_scores, query_heads, preferred_element_ty...  8.97 us
  transfers between devices with their start and end apart: 5, of which 5 were waited for; matrix products, arithmetic and copies ran while one was open for 3% of the time, Pallas kernels for 0%

commit v1 on v0

v1 whole, which is shorter than its diff:
```python
import jax
import jax.numpy as jnp
from jax import lax
from jax.experimental import pallas as pl
from jax.experimental.pallas import tpu as pltpu
from jax.sharding import Mesh, PartitionSpec as P

HEADS = 32
HD = 64
INV_TEMP = 8.0
DISTILL = 128.0
UNROLL = 4
VMEM_LIMIT = 48 * 1024 * 1024
F32 = jnp.float32
BF16 = jnp.bfloat16
NT = (((1,), (1,)), ((), ()))
TN = (((0,), (0,)), ((), ()))


def shift(x, axis, step):
    size = lax.axis_size(axis)
    return lax.ppermute(x, axis, [(i, (i + step) % size) for i in range(size)])


def swap(x, axis, bit):
    size = lax.axis_size(axis)
    return lax.ppermute(x, axis, [(i, i ^ bit) for i in range(size)])


def head_masks(rows, cols):
    lane = lax.broadcasted_iota(jnp.int32, (rows, cols), 1)
    return [lane // HD == h for h in range(cols // HD)]


def block_diagonal(x, masks):
    zero = jnp.zeros_like(x)
    return jnp.concatenate([jnp.where(m, x, zero) for m in masks], axis=0)


def pair_scores(qb, cb, kv, length, score_scale):
    cols = qb.shape[1]
    scores = lax.dot_general(kv[:, :cols], qb, NT, preferred_element_type=F32) * score_scale
    d_prob = lax.dot_general(kv[:, cols:], cb, NT, preferred_element_type=F32)
    row = lax.broadcasted_iota(jnp.int32, scores.shape, 0)
    return jnp.where(row < length, jnp.exp(scores), 0.0), d_prob


def forward_kernel(count, pair_query, pair_row, pair_len, q_ref, c_ref, kv_ref, sums_ref):
    sums_ref[...] = jnp.zeros_like(sums_ref)
    masks = head_masks(q_ref.shape[1], q_ref.shape[2])
    score_scale = HD ** (-0.5)

    def group(g, carry):
        results = []
        for u in range(UNROLL):
            s = g * UNROLL + u
            qi = pair_query[s]
            qb = block_diagonal(q_ref[qi], masks)
            cb = block_diagonal(c_ref[qi], masks)
            expd, d_prob = pair_scores(qb, cb, kv_ref[pair_row[s]], pair_len[s], score_scale)
            total = jnp.sum(expd, axis=0, keepdims=True)
            safe = jnp.where(total > 0.0, total, 1.0)
            mean = jnp.sum((expd / safe) * d_prob, axis=0, keepdims=True)
            results.append((qi, total, mean))
        for qi, total, mean in results:
            old = sums_ref[qi]
            both = old[:1] + total
            safe = jnp.where(both > 0.0, both, 1.0)
            merged = old[1:] * (old[:1] / safe) + mean * (total / safe)
            sums_ref[qi] = jnp.concatenate([both, merged], axis=0)
        return carry

    lax.fori_loop(0, (count[0] + UNROLL - 1) // UNROLL, group, 0)


def backward_kernel(
    count, pair_query, pair_row, pair_len, q_ref, c_ref, kv_ref, sums_ref,
    dkv_ref, ctx_ref, mass_ref, dkv_acc, ctx_acc,
):
    dkv_acc[...] = jnp.zeros_like(dkv_acc)
    ctx_acc[...] = jnp.zeros_like(ctx_acc)
    mass_ref[...] = jnp.zeros_like(mass_ref)
    cols = q_ref.shape[2]
    masks = head_masks(q_ref.shape[1], cols)
    score_scale = HD ** (-0.5)

    def group(g, carry):
        results = []
        for u in range(UNROLL):
            s = g * UNROLL + u
            qi = pair_query[s]
            row = pair_row[s]
            qb = block_diagonal(q_ref[qi], masks)
            cb = block_diagonal(c_ref[qi], masks)
            kv = kv_ref[row]
            expd, d_prob = pair_scores(qb, cb, kv, pair_len[s], score_scale)
            sums = sums_ref[qi]
            prob = expd / sums[:1]
            prob_b = prob.astype(BF16)
            d_scores = (prob * (d_prob - sums[1:]) * score_scale).astype(BF16)
            key_grad = jnp.dot(d_scores, qb, preferred_element_type=F32)
            value_grad = jnp.dot(prob_b, cb, preferred_element_type=F32)
            full = lax.dot_general(prob_b, kv[:, cols:], TN, preferred_element_type=F32)
            part = jnp.zeros(ctx_acc.shape[1:], F32)
            for h, m in enumerate(masks):
                part = jnp.where(m, full[h * HD : (h + 1) * HD], part)
            results.append((s, qi, row, key_grad, value_grad, part, jnp.sum(prob, axis=0, keepdims=True)))
        for s, qi, row, key_grad, value_grad, part, mass in results:
            dkv_acc[row, :, :cols] += key_grad
            dkv_acc[row, :, cols:] += value_grad
            ctx_acc[qi] += part
            mass_ref[s] = mass
        return carry

    lax.fori_loop(0, (count[0] + UNROLL - 1) // UNROLL, group, 0)
    dkv_ref[...] = dkv_acc[...].astype(BF16)
    ctx_ref[...] = ctx_acc[...].astype(BF16)


def smem():
    return pl.BlockSpec(memory_space=pltpu.SMEM)


def vmem():
    return pl.BlockSpec(memory_space=pltpu.VMEM)


def per_device(queries_vec, retr_query, passages, kv_weight, retrieval, lengths, ctx_cot):
    nz, ny, nx, nc = (lax.axis_size(a) for a in ("z", "y", "x", "core"))
    z, y, x, core = (lax.axis_index(a) for a in ("z", "y", "x", "core"))
    own_count, token_count, local_width = passages.shape
    full_width = kv_weight.shape[0]
    head_cols = kv_weight.shape[2]
    query_count, query_tokens, _ = queries_vec.shape
    picks = retrieval.shape[1]
    width_scale = INV_TEMP * full_width ** (-0.5)
    tokens = own_count * token_count
    kv_cols = 2 * head_cols
    meet_queries = nz * query_count
    meet_rows = ny * own_count
    cap = 2 * nz * ny

    with jax.named_scope("gather_queries"):
        packed = jnp.concatenate(
            [queries_vec, ctx_cot, retr_query.reshape(query_count, -1, head_cols)], axis=1
        )
        met = lax.all_gather(packed, "z", axis=0, tiled=True)
        q_all = met[:, :query_tokens]
        c_all = met[:, query_tokens : 2 * query_tokens]
        rq_all = met[:, 2 * query_tokens :].reshape(meet_queries, local_width)

    with jax.named_scope("project"):
        weight = kv_weight.reshape(full_width, kv_cols)
        blocks = weight.reshape(nx, nc, local_width, kv_cols)

        def weight_block(dx, dc):
            return blocks[(x + dx) % nx, (core + dc) % nc]

        own = passages.reshape(tokens, local_width)
        half = tokens // 2
        left = shift(own, "x", 1)
        right = shift(own, "x", -1)
        own_s = swap(own, "core", 1)
        opp_a = shift(left[:half], "x", 1)
        opp_b = shift(right[half:], "x", -1)
        left_s = swap(left, "core", 1)
        right_s = swap(right, "core", 1)
        opp = jnp.concatenate([opp_a, opp_b], axis=0)
        opp_s = swap(opp, "core", 1)
        acc = jnp.dot(own, weight_block(0, 0), preferred_element_type=F32)
        for part, dx, dc in (
            (own_s, 0, 1), (left, -1, 0), (right, 1, 0), (left_s, -1, 1),
            (right_s, 1, 1), (opp, 2, 0), (opp_s, 2, 1),
        ):
            acc = acc + jnp.dot(part, weight_block(dx, dc), preferred_element_type=F32)
        kv = acc.astype(BF16)

    with jax.named_scope("pool"):
        own_id = z * ny + y
        own_lengths = lax.dynamic_slice_in_dim(lengths, own_id * own_count, own_count)
        positions = jnp.arange(token_count, dtype=jnp.int32)
        own_valid = positions[None, :] < own_lengths[:, None]
        own_len_f = own_lengths.astype(F32)
        pooled = jnp.einsum("pt,ptd->pd", own_valid.astype(BF16), passages, preferred_element_type=F32)
        pooled = (pooled / own_len_f[:, None]).astype(BF16)
        pooled_all = jnp.concatenate([pooled] + [shift(pooled, "y", j) for j in range(1, ny)], axis=0)

    with jax.named_scope("pairs"):
        column = lax.dynamic_index_in_dim(
            retrieval.reshape(nz, ny, query_count, picks), y, axis=1, keepdims=False
        ).reshape(meet_queries * picks)
        flat = jnp.arange(meet_queries * picks, dtype=jnp.int32)
        owner = column // own_count
        chosen = owner // ny == z
        row_of = ((y - owner % ny) % ny) * own_count + column % own_count
        rank = jnp.sum((chosen[None, :] & (flat[None, :] < flat[:, None])).astype(jnp.int32), axis=1)
        slots = jnp.arange(cap, dtype=jnp.int32)
        hot = (rank[None, :] == slots[:, None]) & chosen[None, :]
        pick = lambda v: jnp.sum(jnp.where(hot, v[None, :], 0), axis=1)
        pair_query = pick(flat // picks)
        pair_row = pick(row_of)
        pair_len = pick(lengths[column])
        count = jnp.sum(chosen.astype(jnp.int32)).reshape(1)
        met_rows = jnp.arange(meet_rows, dtype=jnp.int32)
        met_queries = jnp.arange(meet_queries, dtype=jnp.int32)
        dense = (
            (pair_query[:, None, None] == met_queries[None, :, None])
            & (pair_row[:, None, None] == met_rows[None, None, :])
            & (slots < count[0])[:, None, None]
        )
        is_pair = jnp.any(dense, axis=0)

    with jax.named_scope("gather_rows"):
        left = shift(kv, "y", 1)
        right = shift(kv, "y", -1)
        opp_a = shift(left[:half], "y", 1)
        opp_b = shift(right[half:], "y", -1)
        kv_all = jnp.concatenate([kv, left, opp_a, opp_b, right], axis=0)
        kv_all = kv_all.reshape(meet_rows, token_count, kv_cols)

    params = pltpu.CompilerParams(vmem_limit_bytes=VMEM_LIMIT)
    with jax.named_scope("forward"):
        part_sums = pl.pallas_call(
            forward_kernel,
            out_shape=jax.ShapeDtypeStruct((meet_queries, 2, head_cols), F32),
            in_specs=[smem()] * 4 + [vmem()] * 3,
            out_specs=vmem(),
            compiler_params=params,
        )(count, pair_query, pair_row, pair_len, q_all, c_all, kv_all)

    with jax.named_scope("exchange"):
        got = lax.all_to_all(
            part_sums.reshape(nz, query_count, 2, head_cols), "z", split_axis=0, concat_axis=0, tiled=True
        )
        total = jnp.sum(got[:, :, 0], axis=0)
        delta = jnp.sum(got[:, :, 1] * (got[:, :, 0] / total[None]), axis=0)
        mine = jnp.stack([total, delta], axis=1)
        sums = lax.all_to_all(
            jnp.broadcast_to(mine[None], (nz,) + mine.shape), "z", split_axis=0, concat_axis=0, tiled=True
        ).reshape(meet_queries, 2, head_cols)

    with jax.named_scope("backward"):
        dkv, ctx_part, mass_rows = pl.pallas_call(
            backward_kernel,
            out_shape=(
                jax.ShapeDtypeStruct((meet_rows, token_count, kv_cols), BF16),
                jax.ShapeDtypeStruct((meet_queries, query_tokens, head_cols), BF16),
                jax.ShapeDtypeStruct((cap, 1, head_cols), F32),
            ),
            in_specs=[smem()] * 4 + [vmem()] * 4,
            out_specs=(vmem(), vmem(), vmem()),
            scratch_shapes=[
                pltpu.VMEM((meet_rows, token_count, kv_cols), F32),
                pltpu.VMEM((meet_queries, query_tokens, head_cols), F32),
            ],
            compiler_params=params,
        )(count, pair_query, pair_row, pair_len, q_all, c_all, kv_all, sums)

    with jax.named_scope("context"):
        context = lax.psum_scatter(ctx_part, "z", scatter_dimension=0, tiled=True)

    with jax.named_scope("return_rows"):
        p0, p3, p2, p1 = (dkv[j * own_count : (j + 1) * own_count].reshape(tokens, kv_cols) for j in range(ny))
        got_a = shift(p2[:half], "y", 1)
        got_b = shift(p2[half:], "y", -1)
        up = jnp.concatenate([p1[:half] + got_a, p1[half:]], axis=0)
        down = jnp.concatenate([p3[:half], p3[half:] + got_b], axis=0)
        got_u = shift(up, "y", 1)
        got_d = shift(down, "y", -1)
        grad_rows = (p0.astype(F32) + got_u.astype(F32) + got_d.astype(F32)).astype(BF16)

    with jax.named_scope("weights_back"):
        def block(dx, dc):
            return lax.dot_general(grad_rows, weight_block(dx, dc), NT, preferred_element_type=F32)

        def both_cores(dx):
            other = swap(block(dx, 1).astype(BF16), "core", 1)
            return block(dx, 0), other

        m2, o2 = both_cores(2)
        s2 = (m2 + o2.astype(F32)).astype(BF16)
        far_a = shift(s2[:half], "x", 1)
        far_b = shift(s2[half:], "x", -1)
        m1, o1 = both_cores(1)
        s1 = m1 + o1.astype(F32)
        m3, o3 = both_cores(-1)
        s3 = m3 + o3.astype(F32)
        m0, o0 = both_cores(0)
        up = jnp.concatenate([s1[:half] + far_a.astype(F32), s1[half:]], axis=0).astype(BF16)
        down = jnp.concatenate([s3[:half], s3[half:] + far_b.astype(F32)], axis=0).astype(BF16)
        got_u = shift(up, "x", 1)
        got_d = shift(down, "x", -1)
        reader_grad = m0 + o0.astype(F32) + got_u.astype(F32) + got_d.astype(F32)

    with jax.named_scope("distill"):
        score_part = jnp.einsum("qd,pd->qp", rq_all, pooled_all, preferred_element_type=F32)
        mass_pair = jnp.sum(mass_rows, axis=(1, 2))
        mass_part = jnp.sum(jnp.where(dense, mass_pair[:, None, None], 0.0), axis=0)
        both = jnp.stack([score_part, mass_part])
        both = both + swap(both, "core", 1)
        both = both + swap(both, "x", 1)
        both = both + swap(both, "x", 2)
        score = both[0] * width_scale
        mass = both[1] / (HEADS * query_tokens)
        log_mass = jnp.log(jnp.where(is_pair, mass, 1.0))
        stats = jnp.stack([
            jnp.sum(jnp.where(is_pair, jnp.exp(score), 0.0), axis=1),
            jnp.sum(jnp.where(is_pair, mass * (log_mass - score), 0.0), axis=1),
            jnp.sum(jnp.where(is_pair, mass, 0.0), axis=1),
        ])
        for bit in (1, 2, 4):
            stats = stats + swap(stats, "z", bit)
        log_total = jnp.log(stats[0])
        divergence = lax.dynamic_slice_in_dim(stats[1] + log_total * stats[2], z * query_count, query_count)
        d_score = DISTILL * (jnp.exp(score - log_total[:, None]) - mass)
        d_score = jnp.where(is_pair, d_score * width_scale, 0.0)
        pool_part = jnp.einsum(
            "qp,qd->pd", d_score, rq_all.astype(F32), precision=lax.Precision.HIGHEST,
            preferred_element_type=F32,
        ).reshape(ny, own_count, local_width)
        grad_pool = pool_part[0]
        for j in range(1, ny):
            grad_pool = grad_pool + shift(pool_part[j], "y", -j)
        retr_grad = own_valid.astype(F32)[:, :, None] / own_len_f[:, None, None] * grad_pool[:, None, :]

    grad_passages = (reader_grad.reshape(passages.shape) + retr_grad).astype(BF16)
    return (context, divergence, grad_passages)


def solution(mesh):
    grid = Mesh(mesh.devices.reshape(8, 4, 4, 2), ("z", "y", "x", "core"))
    dp, mp = ("z", "y"), ("x", "core")
    in_specs = (
        P(dp, None, mp),
        P(dp, mp),
        P(dp, None, mp),
        P(None, None, mp),
        P(),
        P(),
        P(dp, None, mp),
    )
    out_specs = (P(dp, None, mp), P(dp), P(dp, None, mp))
    return jax.shard_map(
        per_device, mesh=grid, in_specs=in_specs, out_specs=out_specs, check_vma=False
    )
```

time: 402 us -> 209 us (0.52)
  blocking collectives: 117 us -> 0 us
  waiting for transfers between devices: 149 us -> 66.2 us
  starting transfers between devices: 20.5 us -> 63.6 us
  local copies, waits for them, and re-layouts: 55 us -> 19.7 us
  Pallas kernels: 0 us -> 18.5 us
  matrix products: 28.4 us -> 14 us
  other arithmetic: 16.3 us -> 9.44 us
    all_to_all x1 -> x0, blocking collectives: 102 us -> none  [per_device(): lax.all_to_all(back_rows, 'dp', split_axis=0, concat_axis=0, tiled=True)]
    all_to_all x3 -> x2, waiting for transfers between devices: 108 us -> 12.6 us  [the longest x1 6.94 us: per_device(): lax.all_to_all(jnp.broadcast_to(mine[None], (nz,) + mine.shape), 'z', spl...]
    ppermute x0 -> x36, waiting for transfers between devices: none -> 53.6 us  [the longest x22 38 us: shift(): return lax.ppermute(x, axis, [(i, (i + step) % size) for i in range(size)])]
    ppermute x0 -> x36, starting transfers between devices: none -> 51.5 us  [the longest x22 32.2 us: shift(): return lax.ppermute(x, axis, [(i, (i + step) % size) for i in range(size)])]
    all_gather x1, waiting for transfers between devices: 38.4 us -> 0.02 us  [per_device(): met = lax.all_gather(packed, 'z', axis=0, tiled=True)]
    pallas_call x0 -> x2, Pallas kernels: none -> 18.5 us  [the longest x1 12.6 us: per_device(): pl.pallas_call(backward_kernel, out_shape=(jax.ShapeDtypeStruct((meet_row...]
    psum x1 -> x0, blocking collectives: 14.9 us -> none  [per_device(): mass_sum = lax.psum(mass_part, 'mp')]
    dot_general x11 -> x19, matrix products: 28.4 us -> 14 us  [the longest x7 5.99 us: per_device(): acc = acc + jnp.dot(part, weight_block(dx, dc), preferred_element_type=F32)]
  transfers between devices with their start and end apart: 5 -> 40, of which waited for: 5 -> 18; matrix products, arithmetic and copies ran while one was open for 3% -> 18% of each run, Pallas kernels for 0% -> 3%
where the time goes in v1:
time: 209 us; the launch traced here: 206 us
  waiting for transfers between devices  66.2 us (32%)
  starting transfers between devices  63.6 us (30%)
  local copies, waits for them, and re-layouts  19.7 us (9%)
  Pallas kernels  18.5 us (9%)
  between operations  14.8 us (7%)
  matrix products  14 us (7%)
  other arithmetic  9.44 us (5%)
    ppermute x22, waiting for transfers between devices, shift(): return lax.ppermute(x, axis, [(i, (i + step) % size) for i in range(size)])  38 us
    ppermute x22, starting transfers between devices, shift(): return lax.ppermute(x, axis, [(i, (i + step) % size) for i in range(size)])  32.2 us
    ppermute x14, starting transfers between devices, swap(): return lax.ppermute(x, axis, [(i, i ^ bit) for i in range(size)])  19.3 us
    ppermute x14, waiting for transfers between devices, swap(): return lax.ppermute(x, axis, [(i, i ^ bit) for i in range(size)])  15.6 us
    pallas_call x1, Pallas kernels, per_device(): pl.pallas_call(backward_kernel, out_shape=(jax.ShapeDtypeStruct((meet_row...  12.6 us
    all_to_all x1, starting transfers between devices, per_device(): lax.all_to_all(part_sums.reshape(nz, query_count, 2, head_cols), 'z', spl...  8.68 us
    reshape x1, local copies, waits for them, and re-layouts, per_device(): blocks = weight.reshape(nx, nc, local_width, kv_cols)  7.66 us
    all_to_all x1, waiting for transfers between devices, per_device(): lax.all_to_all(jnp.broadcast_to(mine[None], (nz,) + mine.shape), 'z', spl...  6.94 us
  transfers between devices with their start and end apart: 40, of which 18 were waited for; matrix products, arithmetic and copies ran while one was open for 18% of the time, Pallas kernels for 3%

profile of v1, /device:TPU:1, one launch (start us, length us, event | category | flops | bytes accessed | tf_op | source)
XLA Modules:
  0.0 206.1 jit_solution(1584291923911036775)
XLA Ops:
  9.3 3.6 %collective-permute-start.14 = (bf16[8,512]{1,0:T(8,128)(2,1)S(1)}, bf16[8,512]{1,0:T(8,128)(2,1)S(1)}, u32[]{:S(2)}, u32[]{:S(2)}) collective-permute-start(bf16[8,512]{1,0:T(8,128)(2,1)S(1)} %fusion.75), channel_id=1, source_target_pairs={{0,24},{8,0},{16,8},{24,16},{1,25},{9,1},{17,9},{25,17},{2,26},{10... | collective-permute-start | bytes 24584 | tf_op jit(solution)/shard_map/pool/ppermute | solution.py:22
  13.3 2.5 %collective-permute-start.2 = (bf16[512,512]{1,0:T(8,128)(2,1)}, bf16[512,512]{1,0:T(8,128)(2,1)S(1)}, u32[]{:S(2)}, u32[]{:S(2)}) collective-permute-start(bf16[512,512]{1,0:T(8,128)(2,1)} %bitcast.157), channel_id=1, source_target_pairs={{0,6},{2,0},{4,2},{6,4},{1,7},{3,1},{5,3},{7,5},{8,14},{10,8},{12,... | collective-permute-start | bytes 1572872 | tf_op jit(solution)/shard_map/project/ppermute | solution.py:22
  20.5 7.7 %reshape.323 = bf16[4,2,512,512]{3,2,1,0:T(8,128)(2,1)} reshape(bf16[4096,2,256]{2,1,0:T(2,128)(2,1)} %param.10) | data formatting | bytes 8388608 | tf_op jit(solution)/shard_map/project/reshape;project/reshape | solution.py:154
  30.7 3.0 %collective-permute-start.6 = (bf16[256,512]{1,0:T(8,128)(2,1)S(1)}, bf16[256,512]{1,0:T(8,128)(2,1)S(1)}, u32[]{:S(2)}, u32[]{:S(2)}) collective-permute-start(bf16[256,512]{1,0:T(8,128)(2,1)S(1)} %slice.169), channel_id=1, source_target_pairs={{0,6},{2,0},{4,2},{6,4},{1,7},{3,1},{5,3},{7,5},{8,14},{10,8},{12,... | collective-permute-start | bytes 786440 | tf_op jit(solution)/shard_map/project/ppermute | solution.py:22
  37.7 5.1 %collective-permute-done.5 = bf16[256,512]{1,0:T(8,128)(2,1)S(1)} collective-permute-done((bf16[256,512]{1,0:T(8,128)(2,1)S(1)}, bf16[256,512]{1,0:T(8,128)(2,1)S(1)}, u32[]{:S(2)}, u32[]{:S(2)}) %collective-permute-start.5) | collective-permute-done | bytes 262176 | tf_op jit(solution)/shard_map/project/ppermute | solution.py:22
  48.6 2.0 collective-permute-start.10
  50.6 1.9 gather_fusion
  52.9 9.7 %collective-permute-done.10 = bf16[512,512]{1,0:T(8,128)(2,1)S(1)} collective-permute-done((bf16[512,512]{1,0:T(8,128)(2,1)}, bf16[512,512]{1,0:T(8,128)(2,1)S(1)}, u32[]{:S(2)}, u32[]{:S(2)}) %collective-permute-start.10) | collective-permute-done | bytes 524320 | tf_op jit(solution)/shard_map/gather_rows/ppermute | solution.py:22
  62.6 2.9 %collective-permute-start.11 = (bf16[256,512]{1,0:T(8,128)(2,1)S(1)}, bf16[256,512]{1,0:T(8,128)(2,1)S(1)}, u32[]{:S(2)}, u32[]{:S(2)}) collective-permute-start(bf16[256,512]{1,0:T(8,128)(2,1)S(1)} %slice.171), channel_id=1, source_target_pairs={{0,24},{8,0},{16,8},{24,16},{1,25},{9,1},{17,9},{25,17},{2,26},{10... | collective-permute-start | bytes 786440 | tf_op jit(solution)/shard_map/gather_rows/ppermute | solution.py:22
  65.6 7.6 %collective-permute-done.9 = bf16[256,512]{1,0:T(8,128)(2,1)S(1)} collective-permute-done((bf16[256,512]{1,0:T(8,128)(2,1)S(1)}, bf16[256,512]{1,0:T(8,128)(2,1)S(1)}, u32[]{:S(2)}, u32[]{:S(2)}) %collective-permute-start.9) | collective-permute-done | bytes 262176 | tf_op jit(solution)/shard_map/gather_rows/ppermute | solution.py:22
  73.4 2.5 %fusion.122 = (bf16[32,64,256]{2,1,0:T(8,128)(2,1)S(1)}, bf16[32,64,256]{2,1,0:T(8,128)(2,1)S(1)}) fusion(bf16[32,130,256]{2,1,0:T(8,128)(2,1)} %all-gather.2.cloned.1.call-done), kind=kLoop, calls=%fused_computation.219 | loop fusion | bytes 4194304 | tf_op jit(solution)/shard_map/gather_queries/slice | solution.py:149
  75.9 5.8 %forward.1 = f32[32,2,256]{2,1,0:T(2,128)} custom-call(s32[1]{0:T(128)} %bitcast.1.count, s32[64]{0:T(128)S(1)} %get-tuple-element.14.pair_query, s32[64]{0:T(128)S(1)} %get-tuple-element.13.pair_row, s32[64]{0:T(128)S(1)} %get-tuple-element.12.pair_len, bf16[32,64,256]{2,1,0:T(8,128)(2,1)S(1)} %get-tuple-element.22.q_ref, ...), custom_call_target="tpu_custom_call" | custom-call | tf_op jit(solution)/shard_map/forward/pallas_call | solution.py:223
  82.8 8.7 %all-to-all-start = ((f32[8,4,2,256]{3,2,1,0:T(2,128)}), f32[8,4,2,256]{3,2,1,0:T(2,128)S(1)}, u32[]{:S(2)}, u32[]{:S(2)}) async-start(f32[8,4,2,256]{3,2,1,0:T(2,128)} %bitcast.14), calls=%async_computation | async-start | bytes 131072 | tf_op jit(solution)/shard_map/exchange/all_to_all | solution.py:232
  93.1 5.6 %all-to-all-done = f32[8,4,2,256]{3,2,1,0:T(2,128)S(1)} async-done(((f32[8,4,2,256]{3,2,1,0:T(2,128)}), f32[8,4,2,256]{3,2,1,0:T(2,128)S(1)}, u32[]{:S(2)}, u32[]{:S(2)}) %all-to-all-start) | async-done | bytes 65568 | tf_op jit(solution)/shard_map/exchange/all_to_all | solution.py:232
  99.5 3.4 %all-to-all-start.1 = ((f32[8,4,2,256]{3,2,1,0:T(2,128)}), f32[8,4,2,256]{3,2,1,0:T(2,128)S(1)}, u32[]{:S(2)}, u32[]{:S(2)}) async-start(f32[8,4,2,256]{3,2,1,0:T(2,128)} %broadcast_in_dim.82), calls=%async_computation.1 | async-start | bytes 131072 | tf_op jit(solution)/shard_map/exchange/all_to_all | solution.py:238
  103.0 6.9 %all-to-all-done.1 = f32[8,4,2,256]{3,2,1,0:T(2,128)S(1)} async-done(((f32[8,4,2,256]{3,2,1,0:T(2,128)}), f32[8,4,2,256]{3,2,1,0:T(2,128)S(1)}, u32[]{:S(2)}, u32[]{:S(2)}) %all-to-all-start.1) | async-done | bytes 65568 | tf_op jit(solution)/shard_map/exchange/all_to_all | solution.py:238
  111.2 12.6 %backward.1 = (bf16[32,64,512]{2,1,0:T(8,128)(2,1)S(1)}, bf16[32,64,256]{2,1,0:T(8,128)(2,1)}, f32[64,1,256]{2,1,0:T(1,128)S(1)}) custom-call(s32[1]{0:T(128)} %bitcast.1.count, s32[64]{0:T(128)S(1)} %get-tuple-element.14.pair_query, s32[64]{0:T(128)S(1)} %get-tuple-element.13.pair_row, s32[64]{0:T(128)S(1)} %get-tuple-element.12.pair_len, ...), custom_call_target="tpu_custom_call" | custom-call | tf_op jit(solution)/shard_map/backward/pallas_call | solution.py:243
  124.7 4.9 %collective-permute-start.15 = (f32[2,32,32]{1,2,0:T(8,128)S(1)}, f32[2,32,32]{1,2,0:T(8,128)S(1)}, u32[]{:S(2)}, u32[]{:S(2)}) collective-permute-start(f32[2,32,32]{1,2,0:T(8,128)S(1)} %pad_maximum_fusion.5), channel_id=1, source_target_pairs={{0,1},{1,0},{2,3},{3,2},{4,5},{5,4},{6,7},{7,6},{8,9},{9,8},{10,11... | collective-permute-start | bytes 24584 | tf_op jit(solution)/shard_map/distill/ppermute | solution.py:27
  130.5 2.8 %collective-permute-done.16 = f32[2,32,32]{1,2,0:T(8,128)S(1)} collective-permute-done((f32[2,32,32]{1,2,0:T(8,128)S(1)}, f32[2,32,32]{1,2,0:T(8,128)S(1)}, u32[]{:S(2)}, u32[]{:S(2)}) %collective-permute-start.16) | collective-permute-done | bytes 8224 | tf_op jit(solution)/shard_map/distill/ppermute | solution.py:27
  134.1 3.5 %collective-permute-done.17 = f32[2,32,32]{1,2,0:T(8,128)S(1)} collective-permute-done((f32[2,32,32]{1,2,0:T(8,128)S(1)}, f32[2,32,32]{1,2,0:T(8,128)S(1)}, u32[]{:S(2)}, u32[]{:S(2)}) %collective-permute-start.17) | collective-permute-done | bytes 8224 | tf_op jit(solution)/shard_map/distill/ppermute | solution.py:27
  137.7 2.6 %collective-permute-start.18 = (f32[3,32]{1,0:T(4,128)S(1)}, f32[3,32]{1,0:T(4,128)S(1)}, u32[]{:S(2)}, u32[]{:S(2)}) collective-permute-start(f32[3,32]{1,0:T(4,128)S(1)} %pad_maximum_fusion.7), channel_id=1, source_target_pairs={{0,32},{32,0},{64,96},{96,64},{128,160},{160,128},{192,224},{224,1... | collective-permute-start | bytes 1160 | tf_op jit(solution)/shard_map/distill/ppermute | solution.py:27
  141.3 3.3 %collective-permute-done.19 = f32[3,32]{1,0:T(4,128)S(1)} collective-permute-done((f32[3,32]{1,0:T(4,128)S(1)}, f32[3,32]{1,0:T(4,128)S(1)}, u32[]{:S(2)}, u32[]{:S(2)}) %collective-permute-start.19) | collective-permute-done | bytes 416 | tf_op jit(solution)/shard_map/distill/ppermute | solution.py:27
  145.1 2.4 %collective-permute-start.23 = (bf16[256,512]{1,0:T(8,128)(2,1)}, bf16[256,512]{1,0:T(8,128)(2,1)S(1)}, u32[]{:S(2)}, u32[]{:S(2)}) collective-permute-start(bf16[256,512]{1,0:T(8,128)(2,1)} %bitcast.163), channel_id=1, source_target_pairs={{0,24},{8,0},{16,8},{24,16},{1,25},{9,1},{17,9},{25,17},{2,26},{10... | collective-permute-start | bytes 786440 | tf_op jit(solution)/shard_map/return_rows/ppermute | solution.py:22
  147.5 3.6 %collective-permute-done.20 = f32[3,32]{1,0:T(4,128)S(1)} collective-permute-done((f32[3,32]{1,0:T(4,128)S(1)}, f32[3,32]{1,0:T(4,128)S(1)}, u32[]{:S(2)}, u32[]{:S(2)}) %collective-permute-start.20) | collective-permute-done | bytes 416 | tf_op jit(solution)/shard_map/distill/ppermute | solution.py:27
  153.4 2.9 %collective-permute-start.24 = (bf16[512,512]{1,0:T(8,128)(2,1)S(1)}, bf16[512,512]{1,0:T(8,128)(2,1)S(1)}, u32[]{:S(2)}, u32[]{:S(2)}) collective-permute-start(bf16[512,512]{1,0:T(8,128)(2,1)S(1)} %pad_maximum_fusion.1), channel_id=1, source_target_pairs={{0,24},{8,0},{16,8},{24,16},{1,25},{9,1},{17,9},{25,17},{2,26},{10... | collective-permute-start | bytes 1572872 | tf_op jit(solution)/shard_map/return_rows/ppermute | solution.py:22
  157.9 4.5 %collective-permute-done.22 = bf16[512,512]{1,0:T(8,128)(2,1)S(1)} collective-permute-done((bf16[512,512]{1,0:T(8,128)(2,1)S(1)}, bf16[512,512]{1,0:T(8,128)(2,1)S(1)}, u32[]{:S(2)}, u32[]{:S(2)}) %collective-permute-start.22) | collective-permute-done | bytes 524320 | tf_op jit(solution)/shard_map/return_rows/ppermute | solution.py:22
  163.1 7.1 %collective-permute-start.26 = (bf16[512,512]{1,0:T(8,128)(2,1)S(1)}, bf16[512,512]{1,0:T(8,128)(2,1)S(1)}, u32[]{:S(2)}, u32[]{:S(2)}) collective-permute-start(bf16[512,512]{1,0:T(8,128)(2,1)S(1)} %convolution_convert_fusion.2), channel_id=1, source_target_pairs={{0,1},{1,0},{2,3},{3,2},{4,5},{5,4},{6,7},{7,6},{8,9},{9,8},{10,11... | collective-permute-start | bytes 1572872 | tf_op jit(solution)/shard_map/weights_back/ppermute | solution.py:27
  174.1 2.7 %collective-permute-start.31 = (bf16[256,512]{1,0:T(8,128)(2,1)S(1)}, bf16[256,512]{1,0:T(8,128)(2,1)S(1)}, u32[]{:S(2)}, u32[]{:S(2)}) collective-permute-start(bf16[256,512]{1,0:T(8,128)(2,1)S(1)} %get-tuple-element.30), channel_id=1, source_target_pairs={{0,6},{2,0},{4,2},{6,4},{1,7},{3,1},{5,3},{7,5},{8,14},{10,8},{12,... | collective-permute-start | bytes 786440 | tf_op jit(solution)/shard_map/weights_back/ppermute | solution.py:22
  177.3 5.6 %collective-permute-done.28 = bf16[256,512]{1,0:T(8,128)(2,1)S(1)} collective-permute-done((bf16[256,512]{1,0:T(8,128)(2,1)S(1)}, bf16[256,512]{1,0:T(8,128)(2,1)S(1)}, u32[]{:S(2)}, u32[]{:S(2)}) %collective-permute-start.28) | collective-permute-done | bytes 262176 | tf_op jit(solution)/shard_map/weights_back/ppermute | solution.py:22
  183.2 2.7 %collective-permute-start.32 = (bf16[512,512]{1,0:T(8,128)(2,1)S(1)}, bf16[512,512]{1,0:T(8,128)(2,1)}, u32[]{:S(2)}, u32[]{:S(2)}) collective-permute-start(bf16[512,512]{1,0:T(8,128)(2,1)S(1)} %pad_maximum_fusion.3), channel_id=1, source_target_pairs={{0,6},{2,0},{4,2},{6,4},{1,7},{3,1},{5,3},{7,5},{8,14},{10,8},{12,... | collective-permute-start | bytes 1572872 | tf_op jit(solution)/shard_map/weights_back/ppermute | solution.py:22
  186.9 3.7 %collective-permute-start.34 = (f32[8,512]{1,0:T(8,128)S(1)}, f32[8,512]{1,0:T(8,128)S(1)}, u32[]{:S(2)}, u32[]{:S(2)}) collective-permute-start(f32[8,512]{1,0:T(8,128)S(1)} %get-tuple-element.33), channel_id=1, source_target_pairs={{0,16},{8,24},{16,0},{24,8},{1,17},{9,25},{17,1},{25,9},{2,18},{10... | collective-permute-start | bytes 49160 | tf_op jit(solution)/shard_map/distill/ppermute | solution.py:22
  191.8 4.7 %collective-permute-done.29 = bf16[512,512]{1,0:T(8,128)(2,1)S(1)} collective-permute-done((bf16[512,512]{1,0:T(8,128)(2,1)S(1)}, bf16[512,512]{1,0:T(8,128)(2,1)S(1)}, u32[]{:S(2)}, u32[]{:S(2)}) %collective-permute-start.29) | collective-permute-done | bytes 524320 | tf_op jit(solution)/shard_map/weights_back/ppermute | solution.py:22
  (159 shorter events, 42.9 us)
Async XLA Ops:
  7.2 66.2 %all-gather.2.cloned.1.call-start = ((), (), s32[]{:S(2)}) async-start(), calls=%async_computation.3 | async-start | bytes 2506752 | tf_op jit(solution)/shard_map/gather_queries/all_gather | solution.py:147
  9.3 93.5 %collective-permute-start.14 = (bf16[8,512]{1,0:T(8,128)(2,1)S(1)}, bf16[8,512]{1,0:T(8,128)(2,1)S(1)}, u32[]{:S(2)}, u32[]{:S(2)}) collective-permute-start(bf16[8,512]{1,0:T(8,128)(2,1)S(1)} %fusion.75), channel_id=1, source_target_pairs={{0,24},{8,0},{16,8},{24,16},{1,25},{9,1},{17,9},{25,17},{2,26},{10... | collective-permute-start | bytes 24584 | tf_op jit(solution)/shard_map/pool/ppermute | solution.py:22
  12.9 90.0 %collective-permute-start.13 = (bf16[8,512]{1,0:T(8,128)(2,1)S(1)}, bf16[8,512]{1,0:T(8,128)(2,1)S(1)}, u32[]{:S(2)}, u32[]{:S(2)}) collective-permute-start(bf16[8,512]{1,0:T(8,128)(2,1)S(1)} %fusion.75), channel_id=1, source_target_pairs={{0,16},{8,24},{16,0},{24,8},{1,17},{9,25},{17,1},{25,9},{2,18},{10... | collective-permute-start | bytes 24584 | tf_op jit(solution)/shard_map/pool/ppermute | solution.py:22
  13.3 17.4 %collective-permute-start.2 = (bf16[512,512]{1,0:T(8,128)(2,1)}, bf16[512,512]{1,0:T(8,128)(2,1)S(1)}, u32[]{:S(2)}, u32[]{:S(2)}) collective-permute-start(bf16[512,512]{1,0:T(8,128)(2,1)} %bitcast.157), channel_id=1, source_target_pairs={{0,6},{2,0},{4,2},{6,4},{1,7},{3,1},{5,3},{7,5},{8,14},{10,8},{12,... | collective-permute-start | bytes 1572872 | tf_op jit(solution)/shard_map/project/ppermute | solution.py:22
  15.7 18.0 %collective-permute-start.1 = (bf16[512,512]{1,0:T(8,128)(2,1)}, bf16[512,512]{1,0:T(8,128)(2,1)S(1)}, u32[]{:S(2)}, u32[]{:S(2)}) collective-permute-start(bf16[512,512]{1,0:T(8,128)(2,1)} %bitcast.158), channel_id=1, source_target_pairs={{0,2},{2,4},{4,6},{6,0},{1,3},{3,5},{5,7},{7,1},{8,10},{10,12},{12... | collective-permute-start | bytes 1572872 | tf_op jit(solution)/shard_map/project/ppermute | solution.py:22
  15.7 19.6 %collective-permute-start = (bf16[512,512]{1,0:T(8,128)(2,1)}, bf16[512,512]{1,0:T(8,128)(2,1)S(1)}, u32[]{:S(2)}, u32[]{:S(2)}) collective-permute-start(bf16[512,512]{1,0:T(8,128)(2,1)} %bitcast.159), channel_id=1, source_target_pairs={{0,1},{1,0},{2,3},{3,2},{4,5},{5,4},{6,7},{7,6},{8,9},{9,8},{10,11... | collective-permute-start | bytes 1572872 | tf_op jit(solution)/shard_map/project/ppermute | solution.py:27
  30.7 12.8 %collective-permute-start.6 = (bf16[256,512]{1,0:T(8,128)(2,1)S(1)}, bf16[256,512]{1,0:T(8,128)(2,1)S(1)}, u32[]{:S(2)}, u32[]{:S(2)}) collective-permute-start(bf16[256,512]{1,0:T(8,128)(2,1)S(1)} %slice.169), channel_id=1, source_target_pairs={{0,6},{2,0},{4,2},{6,4},{1,7},{3,1},{5,3},{7,5},{8,14},{10,8},{12,... | collective-permute-start | bytes 786440 | tf_op jit(solution)/shard_map/project/ppermute | solution.py:22
  33.8 9.0 %collective-permute-start.5 = (bf16[256,512]{1,0:T(8,128)(2,1)S(1)}, bf16[256,512]{1,0:T(8,128)(2,1)S(1)}, u32[]{:S(2)}, u32[]{:S(2)}) collective-permute-start(bf16[256,512]{1,0:T(8,128)(2,1)S(1)} %slice.168), channel_id=1, source_target_pairs={{0,2},{2,4},{4,6},{6,0},{1,3},{3,5},{5,7},{7,1},{8,10},{10,12},{12... | collective-permute-start | bytes 786440 | tf_op jit(solution)/shard_map/project/ppermute | solution.py:22
  35.3 10.0 %collective-permute-start.4 = (bf16[512,512]{1,0:T(8,128)(2,1)S(1)}, bf16[512,512]{1,0:T(8,128)(2,1)S(1)}, u32[]{:S(2)}, u32[]{:S(2)}) collective-permute-start(bf16[512,512]{1,0:T(8,128)(2,1)S(1)} %collective-permute-done.2), channel_id=1, source_target_pairs={{0,1},{1,0},{2,3},{3,2},{4,5},{5,4},{6,7},{7,6},{8,9},{9,8},{10,11... | collective-permute-start | bytes 1572872 | tf_op jit(solution)/shard_map/project/ppermute | solution.py:27
  42.8 60.1 %collective-permute-start.12 = (bf16[8,512]{1,0:T(8,128)(2,1)S(1)}, bf16[8,512]{1,0:T(8,128)(2,1)S(1)}, u32[]{:S(2)}, u32[]{:S(2)}) collective-permute-start(bf16[8,512]{1,0:T(8,128)(2,1)S(1)} %fusion.75), channel_id=1, source_target_pairs={{0,8},{8,16},{16,24},{24,0},{1,9},{9,17},{17,25},{25,1},{2,10},{10... | collective-permute-start | bytes 24584 | tf_op jit(solution)/shard_map/pool/ppermute | solution.py:22
  48.6 13.9 %collective-permute-start.10 = (bf16[512,512]{1,0:T(8,128)(2,1)}, bf16[512,512]{1,0:T(8,128)(2,1)S(1)}, u32[]{:S(2)}, u32[]{:S(2)}) collective-permute-start(bf16[512,512]{1,0:T(8,128)(2,1)} %get-tuple-element.38), channel_id=1, source_target_pairs={{0,24},{8,0},{16,8},{24,16},{1,25},{9,1},{17,9},{25,17},{2,26},{10... | collective-permute-start | bytes 1572872 | tf_op jit(solution)/shard_map/gather_rows/ppermute | solution.py:22
  50.6 14.8 %collective-permute-start.8 = (bf16[512,512]{1,0:T(8,128)(2,1)}, bf16[512,512]{1,0:T(8,128)(2,1)S(1)}, u32[]{:S(2)}, u32[]{:S(2)}) collective-permute-start(bf16[512,512]{1,0:T(8,128)(2,1)} %get-tuple-element.38), channel_id=1, source_target_pairs={{0,8},{8,16},{16,24},{24,0},{1,9},{9,17},{17,25},{25,1},{2,10},{10... | collective-permute-start | bytes 1572872 | tf_op jit(solution)/shard_map/gather_rows/ppermute | solution.py:22
  62.6 10.7 %collective-permute-start.11 = (bf16[256,512]{1,0:T(8,128)(2,1)S(1)}, bf16[256,512]{1,0:T(8,128)(2,1)S(1)}, u32[]{:S(2)}, u32[]{:S(2)}) collective-permute-start(bf16[256,512]{1,0:T(8,128)(2,1)S(1)} %slice.171), channel_id=1, source_target_pairs={{0,24},{8,0},{16,8},{24,16},{1,25},{9,1},{17,9},{25,17},{2,26},{10... | collective-permute-start | bytes 786440 | tf_op jit(solution)/shard_map/gather_rows/ppermute | solution.py:22
  65.5 7.8 %collective-permute-start.9 = (bf16[256,512]{1,0:T(8,128)(2,1)S(1)}, bf16[256,512]{1,0:T(8,128)(2,1)S(1)}, u32[]{:S(2)}, u32[]{:S(2)}) collective-permute-start(bf16[256,512]{1,0:T(8,128)(2,1)S(1)} %slice.170), channel_id=1, source_target_pairs={{0,8},{8,16},{16,24},{24,0},{1,9},{9,17},{17,25},{25,1},{2,10},{10... | collective-permute-start | bytes 786440 | tf_op jit(solution)/shard_map/gather_rows/ppermute | solution.py:22
  82.8 15.9 %all-to-all-start = ((f32[8,4,2,256]{3,2,1,0:T(2,128)}), f32[8,4,2,256]{3,2,1,0:T(2,128)S(1)}, u32[]{:S(2)}, u32[]{:S(2)}) async-start(f32[8,4,2,256]{3,2,1,0:T(2,128)} %bitcast.14), calls=%async_computation | async-start | bytes 131072 | tf_op jit(solution)/shard_map/exchange/all_to_all | solution.py:232
  99.5 10.5 %all-to-all-start.1 = ((f32[8,4,2,256]{3,2,1,0:T(2,128)}), f32[8,4,2,256]{3,2,1,0:T(2,128)S(1)}, u32[]{:S(2)}, u32[]{:S(2)}) async-start(f32[8,4,2,256]{3,2,1,0:T(2,128)} %broadcast_in_dim.82), calls=%async_computation.1 | async-start | bytes 131072 | tf_op jit(solution)/shard_map/exchange/all_to_all | solution.py:238
  102.8 96.4 %reduce-scatter.2.cloned.1.call-start = ((), (), s32[]{:S(2)}) async-start(), calls=%async_computation.4 | async-start | bytes 1179648 | tf_op jit(solution)/shard_map/context/reduce_scatter | solution.py:260
  124.7 5.7 %collective-permute-start.15 = (f32[2,32,32]{1,2,0:T(8,128)S(1)}, f32[2,32,32]{1,2,0:T(8,128)S(1)}, u32[]{:S(2)}, u32[]{:S(2)}) collective-permute-start(f32[2,32,32]{1,2,0:T(8,128)S(1)} %pad_maximum_fusion.5), channel_id=1, source_target_pairs={{0,1},{1,0},{2,3},{3,2},{4,5},{5,4},{6,7},{7,6},{8,9},{9,8},{10,11... | collective-permute-start | bytes 24584 | tf_op jit(solution)/shard_map/distill/ppermute | solution.py:27
  141.1 10.0 %collective-permute-start.21 = (bf16[256,512]{1,0:T(8,128)(2,1)}, bf16[256,512]{1,0:T(8,128)(2,1)}, u32[]{:S(2)}, u32[]{:S(2)}) collective-permute-start(bf16[256,512]{1,0:T(8,128)(2,1)} %bitcast.31), channel_id=1, source_target_pairs={{0,8},{8,16},{16,24},{24,0},{1,9},{9,17},{17,25},{25,1},{2,10},{10... | collective-permute-start | bytes 786440 | tf_op jit(solution)/shard_map/return_rows/ppermute | solution.py:22
  144.7 6.4 %collective-permute-start.20 = (f32[3,32]{1,0:T(4,128)S(1)}, f32[3,32]{1,0:T(4,128)S(1)}, u32[]{:S(2)}, u32[]{:S(2)}) collective-permute-start(f32[3,32]{1,0:T(4,128)S(1)} %fusion.145), channel_id=1, source_target_pairs={{0,128},{32,160},{64,192},{96,224},{128,0},{160,32},{192,64},{224,... | collective-permute-start | bytes 1160 | tf_op jit(solution)/shard_map/distill/ppermute | solution.py:27
  145.1 8.2 %collective-permute-start.23 = (bf16[256,512]{1,0:T(8,128)(2,1)}, bf16[256,512]{1,0:T(8,128)(2,1)S(1)}, u32[]{:S(2)}, u32[]{:S(2)}) collective-permute-start(bf16[256,512]{1,0:T(8,128)(2,1)} %bitcast.163), channel_id=1, source_target_pairs={{0,24},{8,0},{16,8},{24,16},{1,25},{9,1},{17,9},{25,17},{2,26},{10... | collective-permute-start | bytes 786440 | tf_op jit(solution)/shard_map/return_rows/ppermute | solution.py:22
  153.1 9.3 %collective-permute-start.22 = (bf16[512,512]{1,0:T(8,128)(2,1)S(1)}, bf16[512,512]{1,0:T(8,128)(2,1)S(1)}, u32[]{:S(2)}, u32[]{:S(2)}) collective-permute-start(bf16[512,512]{1,0:T(8,128)(2,1)S(1)} %pad_maximum_fusion), channel_id=1, source_target_pairs={{0,8},{8,16},{16,24},{24,0},{1,9},{9,17},{17,25},{25,1},{2,10},{10... | collective-permute-start | bytes 1572872 | tf_op jit(solution)/shard_map/return_rows/ppermute | solution.py:22
  153.4 9.0 %collective-permute-start.24 = (bf16[512,512]{1,0:T(8,128)(2,1)S(1)}, bf16[512,512]{1,0:T(8,128)(2,1)S(1)}, u32[]{:S(2)}, u32[]{:S(2)}) collective-permute-start(bf16[512,512]{1,0:T(8,128)(2,1)S(1)} %pad_maximum_fusion.1), channel_id=1, source_target_pairs={{0,24},{8,0},{16,8},{24,16},{1,25},{9,1},{17,9},{25,17},{2,26},{10... | collective-permute-start | bytes 1572872 | tf_op jit(solution)/shard_map/return_rows/ppermute | solution.py:22
  156.4 30.5 %collective-permute-start.33 = (f32[8,512]{1,0:T(8,128)S(1)}, f32[8,512]{1,0:T(8,128)S(1)}, u32[]{:S(2)}, u32[]{:S(2)}) collective-permute-start(f32[8,512]{1,0:T(8,128)S(1)} %get-tuple-element.31), channel_id=1, source_target_pairs={{0,24},{8,0},{16,8},{24,16},{1,25},{9,1},{17,9},{25,17},{2,26},{10... | collective-permute-start | bytes 49160 | tf_op jit(solution)/shard_map/distill/ppermute | solution.py:22
  163.1 9.4 %collective-permute-start.26 = (bf16[512,512]{1,0:T(8,128)(2,1)S(1)}, bf16[512,512]{1,0:T(8,128)(2,1)S(1)}, u32[]{:S(2)}, u32[]{:S(2)}) collective-permute-start(bf16[512,512]{1,0:T(8,128)(2,1)S(1)} %convolution_convert_fusion.2), channel_id=1, source_target_pairs={{0,1},{1,0},{2,3},{3,2},{4,5},{5,4},{6,7},{7,6},{8,9},{9,8},{10,11... | collective-permute-start | bytes 1572872 | tf_op jit(solution)/shard_map/weights_back/ppermute | solution.py:27
  170.7 21.1 %collective-permute-start.25 = (bf16[512,512]{1,0:T(8,128)(2,1)S(1)}, bf16[512,512]{1,0:T(8,128)(2,1)S(1)}, u32[]{:S(2)}, u32[]{:S(2)}) collective-permute-start(bf16[512,512]{1,0:T(8,128)(2,1)S(1)} %convolution_convert_fusion.3), channel_id=1, source_target_pairs={{0,1},{1,0},{2,3},{3,2},{4,5},{5,4},{6,7},{7,6},{8,9},{9,8},{10,11... | collective-permute-start | bytes 1572872 | tf_op jit(solution)/shard_map/weights_back/ppermute | solution.py:27
  174.0 8.9 %collective-permute-start.28 = (bf16[256,512]{1,0:T(8,128)(2,1)S(1)}, bf16[256,512]{1,0:T(8,128)(2,1)S(1)}, u32[]{:S(2)}, u32[]{:S(2)}) collective-permute-start(bf16[256,512]{1,0:T(8,128)(2,1)S(1)} %get-tuple-element.29), channel_id=1, source_target_pairs={{0,2},{2,4},{4,6},{6,0},{1,3},{3,5},{5,7},{7,1},{8,10},{10,12},{12... | collective-permute-start | bytes 786440 | tf_op jit(solution)/shard_map/weights_back/ppermute | solution.py:22
  174.1 9.0 %collective-permute-start.31 = (bf16[256,512]{1,0:T(8,128)(2,1)S(1)}, bf16[256,512]{1,0:T(8,128)(2,1)S(1)}, u32[]{:S(2)}, u32[]{:S(2)}) collective-permute-start(bf16[256,512]{1,0:T(8,128)(2,1)S(1)} %get-tuple-element.30), channel_id=1, source_target_pairs={{0,6},{2,0},{4,2},{6,4},{1,7},{3,1},{5,3},{7,5},{8,14},{10,8},{12,... | collective-permute-start | bytes 786440 | tf_op jit(solution)/shard_map/weights_back/ppermute | solution.py:22
  183.0 13.6 %collective-permute-start.29 = (bf16[512,512]{1,0:T(8,128)(2,1)S(1)}, bf16[512,512]{1,0:T(8,128)(2,1)S(1)}, u32[]{:S(2)}, u32[]{:S(2)}) collective-permute-start(bf16[512,512]{1,0:T(8,128)(2,1)S(1)} %pad_maximum_fusion.2), channel_id=1, source_target_pairs={{0,2},{2,4},{4,6},{6,0},{1,3},{3,5},{5,7},{7,1},{8,10},{10,12},{12... | collective-permute-start | bytes 1572872 | tf_op jit(solution)/shard_map/weights_back/ppermute | solution.py:22
  183.2 13.3 %collective-permute-start.32 = (bf16[512,512]{1,0:T(8,128)(2,1)S(1)}, bf16[512,512]{1,0:T(8,128)(2,1)}, u32[]{:S(2)}, u32[]{:S(2)}) collective-permute-start(bf16[512,512]{1,0:T(8,128)(2,1)S(1)} %pad_maximum_fusion.3), channel_id=1, source_target_pairs={{0,6},{2,0},{4,2},{6,4},{1,7},{3,1},{5,3},{7,5},{8,14},{10,8},{12,... | collective-permute-start | bytes 1572872 | tf_op jit(solution)/shard_map/weights_back/ppermute | solution.py:22
  186.0 5.1 %collective-permute-start.35 = (f32[8,512]{1,0:T(8,128)S(1)}, f32[8,512]{1,0:T(8,128)S(1)}, u32[]{:S(2)}, u32[]{:S(2)}) collective-permute-start(f32[8,512]{1,0:T(8,128)S(1)} %get-tuple-element.32), channel_id=1, source_target_pairs={{0,8},{8,16},{16,24},{24,0},{1,9},{9,17},{17,25},{25,1},{2,10},{10... | collective-permute-start | bytes 49160 | tf_op jit(solution)/shard_map/distill/ppermute | solution.py:22
  186.9 5.0 %collective-permute-start.34 = (f32[8,512]{1,0:T(8,128)S(1)}, f32[8,512]{1,0:T(8,128)S(1)}, u32[]{:S(2)}, u32[]{:S(2)}) collective-permute-start(f32[8,512]{1,0:T(8,128)S(1)} %get-tuple-element.33), channel_id=1, source_target_pairs={{0,16},{8,24},{16,0},{24,8},{1,17},{9,25},{17,1},{25,9},{2,18},{10... | collective-permute-start | bytes 49160 | tf_op jit(solution)/shard_map/distill/ppermute | solution.py:22
  (15 other events, 72.7 us)
Sparse Core Ops, SparseCore 0:
  19.8 40.3 all-gather.1
  145.2 36.9 reduce-scatter.1
